TPU v7x, 32 devices: a whole 2x2x4 slice. The times are simulated.
32 devices in a mesh: leaf: 8 (over z, y), rhs: 4 (over x, core).
Axes of the slice: x: 2, y: 2, z: 4, core: 2. Of those that a mesh axis runs over, the one named last changes fastest.
Arguments:
- excitation: bfloat16 [2, 32, 65536], P(None, 'rhs', 'leaf'), parts along dimension 1, may hold values from -6 to 6
- source_weight: float32 [65536], P('leaf'), may hold values from 0.25 to 4
- tree_order: int32 [65536], P('leaf'), may hold values from 0 to 8191, as said below
- leaf_basis: bfloat16 [2, 64, 64], replicated, may hold values from -0.5 to 0.5
- transfer: bfloat16 [10, 2, 2, 64, 2, 64], replicated, may hold values from -0.375 to 0.375
- eval_basis: bfloat16 [2, 64, 64], replicated, may hold values from -0.5 to 0.5
Outputs:
- out_field: float32 [2, 32, 65536], P(None, 'rhs', 'leaf'), parts along dimension 1
There are 4 independent parts, one for each index of `rhs`. A program takes and returns all parts, laid end to end along the dimension named above; an argument that names none is the same for every part. Nothing has to cross between parts.
Inputs may be any that keep to these rules, and one draw needn't show every extreme that they name: `tree_order`: each aligned block of 8192 entries (the points of one device) holds every number 0 to 8191 once.
All inputs are finite; a program needn't handle non-finite values.
Results may differ from a plain program's by a relative error of at most 0.015.
Values may be sent and summed in bfloat16 or wider, within the bound.
A program may use at most 64 MiB of HBM per device.

v0:
```python
import jax
import jax.numpy as jnp
from jax import lax
from jax.sharding import PartitionSpec as P


def swapped(block, axis, distance):
    count = lax.axis_size(axis)
    route = []
    for low in range(count):
        high = low | 1 << distance
        if high != low and high < count:
            route += [(low, high), (high, low)]
    return lax.ppermute(block, axis, route)


def complex_form(blocks_pair):
    real_part = blocks_pair[0]
    imag_part = blocks_pair[1]
    return jnp.stack([jnp.stack([real_part, -imag_part]), jnp.stack([imag_part, real_part])])


def bit_count(value):
    return value.bit_length() - 1


def run_levels(coeffs, matrices, sources, targets, vec_count):
    coeff_rank = coeffs.shape[1]
    level_count = len(matrices)
    source_bits = bit_count(sources)
    first_count = 0
    while first_count < level_count and (sources >> first_count + 1) * vec_count >= 128:
        first_count += 1
    split_bits = coeffs.reshape((2, coeff_rank) + (2,) * source_bits + (targets, vec_count))
    order = (source_bits + 2, 0, 1) + tuple(range(source_bits + 1, 1, -1)) + (source_bits + 3,)
    state = jnp.transpose(split_bits, order).reshape(targets, 2, coeff_rank, sources * vec_count)
    for level_index in range(first_count):
        forms = complex_form(matrices[level_index])
        lifted = jnp.transpose(forms, (2, 0, 3, 1, 5, 4)).reshape(2, 2 * coeff_rank, 4 * coeff_rank)
        held = state.shape[0]
        columns = state.shape[3] // 2
        stacked = state.reshape(held, 4 * coeff_rank, columns)
        result = jnp.einsum("jmk,tkn->tjmn", lifted, stacked, preferred_element_type=jnp.float32)
        state = result.astype(jnp.bfloat16).reshape(2 * held, 2, coeff_rank, columns)
    held_targets = state.shape[0]
    left_bits = source_bits - first_count
    left_sources = 1 << left_bits
    split_state = state.reshape((held_targets, 2, coeff_rank) + (2,) * left_bits + (vec_count,))
    order = tuple(range(left_bits + 2, 2, -1)) + (1, 2, 0, left_bits + 3)
    state = jnp.transpose(split_state, order).reshape(
        left_sources, 2, coeff_rank, held_targets * vec_count
    )
    second_count = level_count - first_count
    for level_index in range(first_count, level_count):
        forms = complex_form(matrices[level_index])
        lifted = jnp.transpose(forms, (2, 0, 3, 4, 1, 5)).reshape(2, 2 * coeff_rank, 4 * coeff_rank)
        count_now = state.shape[0] // 2
        columns = state.shape[3]
        stacked = state.reshape(count_now, 4 * coeff_rank, columns)
        result = jnp.einsum("jmk,skc->smjc", lifted, stacked, preferred_element_type=jnp.float32)
        state = result.astype(jnp.bfloat16).reshape(count_now, 2, coeff_rank, 2 * columns)
    final_sources = state.shape[0]
    split_state = state.reshape(
        (final_sources, 2, coeff_rank) + (2,) * second_count + (held_targets, vec_count)
    )
    order = (
        (1, 2, 0, second_count + 3) + tuple(range(second_count + 2, 2, -1)) + (second_count + 4,)
    )
    return jnp.transpose(split_state, order).reshape(2, coeff_rank, -1)


def evaluate(eval_basis, coeffs, box_count, vec_count):
    grouped = coeffs.reshape(2, coeffs.shape[1], box_count, vec_count)
    values = jnp.einsum(
        "pqlr,qrtv->pvtl", complex_form(eval_basis), grouped, preferred_element_type=jnp.float32
    )
    return values.reshape(2, vec_count, box_count * eval_basis.shape[1])


def per_device(excitation, source_weight, tree_order, leaf_basis, transfer, eval_basis):
    vec_count = excitation.shape[1]
    point_count = excitation.shape[2]
    leaf_size = leaf_basis.shape[2]
    coeff_rank = leaf_basis.shape[1]
    box_count = point_count // leaf_size
    axis_size = lax.axis_size("leaf")
    cross_levels = axis_size.bit_length() - 1
    local_levels = transfer.shape[0] - cross_levels
    per_peer = box_count // axis_size
    in_tree = jnp.take(excitation, tree_order, axis=2)
    weights_tree = jnp.take(source_weight, tree_order)
    weighted = (in_tree.astype(jnp.float32) * weights_tree).astype(jnp.bfloat16)
    leaf_boxes = weighted.reshape(2, vec_count, box_count, leaf_size)
    coeffs = jnp.einsum(
        "pqrl,qvsl->prsv", complex_form(leaf_basis), leaf_boxes, preferred_element_type=jnp.float32
    )
    coeffs = coeffs.reshape(2, coeff_rank, box_count * vec_count).astype(jnp.bfloat16)
    local_mats = [transfer[level_index] for level_index in range(local_levels)]
    coeffs = run_levels(coeffs, local_mats, box_count, 1, vec_count)
    position = lax.axis_index("leaf")
    for cross_index in range(cross_levels):
        partner = swapped(coeffs, "leaf", cross_index)
        own_bit = position >> cross_index & 1
        matrix = complex_form(transfer[local_levels + cross_index])
        child_matrix = jnp.where(own_bit == 1, matrix[:, :, 1], matrix[:, :, 0])
        own_side = jnp.where(own_bit == 1, child_matrix[:, :, :, 1], child_matrix[:, :, :, 0])
        other_side = jnp.where(own_bit == 1, child_matrix[:, :, :, 0], child_matrix[:, :, :, 1])
        combined = jnp.einsum("pqry,qyw->prw", own_side, coeffs, preferred_element_type=jnp.float32)
        combined = combined + jnp.einsum(
            "pqry,qyw->prw", other_side, partner, preferred_element_type=jnp.float32
        )
        coeffs = combined.astype(jnp.bfloat16)
    axis_order = (
        (0, 1, 2 + cross_levels) + tuple(range(1 + cross_levels, 1, -1)) + (3 + cross_levels,)
    )
    held_values = evaluate(eval_basis, coeffs, box_count, vec_count)
    arrived = lax.all_to_all(
        held_values.astype(jnp.bfloat16), "leaf", split_axis=2, concat_axis=2, tiled=True
    ).astype(held_values.dtype)
    bit_split = arrived.reshape((2, vec_count) + (2,) * cross_levels + (per_peer, leaf_size))
    potential = jnp.transpose(bit_split, axis_order).reshape(2, vec_count, point_count)
    inverse = (
        jnp.zeros((point_count,), jnp.int32)
        .at[tree_order]
        .set(jnp.arange(point_count, dtype=jnp.int32))
    )
    out_field = jnp.take(potential, inverse, axis=2)
    return out_field


def solution(mesh):
    in_specs = (P(None, "rhs", "leaf"), P("leaf"), P("leaf"), P(), P(), P())
    out_specs = P(None, "rhs", "leaf")
    return jax.shard_map(
        per_device, mesh=mesh, in_specs=in_specs, out_specs=out_specs, check_vma=False
    )
```

profile of v0, /device:TPU:0, one launch (start us, length us, event | category | flops | bytes accessed | tf_op | source)
XLA Modules:
  0.0 356.8 jit_solution(4960302710310866192)
XLA Ops:
  0.0 0.9 slice_bitcast_fusion.1
  0.9 1.4 fusion.90
  2.3 2.5 fusion.91
  4.8 0.7 slice_negate_fusion.1
  5.5 0.8 compare_select_fusion.1
  6.3 45.5 %gather_fusion.1 = f32[8192]{0:T(1024)S(1)} fusion(f32[8192]{0:T(1024)S(1)} %copy-done, s32[8192]{0:T(1024)S(1)} %get-tuple-element.54), kind=kCustom, calls=%fused_computation.1 | custom fusion | bytes 98304 | tf_op jit(solution)/shard_map/jit(_take)/gather | solution.py:91
  52.0 0.4 maximum_bitcast_fusion.25
  52.4 0.4 maximum_bitcast_fusion.6
  52.9 0.4 copy.98
  53.5 0.7 maximum_bitcast_fusion.17
  54.2 0.4 maximum_bitcast_fusion.2
  54.7 0.3 copy.86
  55.1 0.4 maximum_bitcast_fusion.3
  55.6 0.4 copy.90
  56.2 0.7 maximum_bitcast_fusion.13
  56.9 0.4 maximum_bitcast_fusion
  57.4 0.3 copy.78
  57.9 0.4 maximum_bitcast_fusion.1
  58.3 0.3 copy.82
  58.8 0.7 maximum_bitcast_fusion.21
  59.5 0.4 maximum_bitcast_fusion.4
  60.0 0.4 copy.92
  60.6 0.4 maximum_bitcast_fusion.5
  61.1 0.4 copy.95
  61.7 6.8 %copy.73 = bf16[2,8,8192]{1,0,2:T(2,128)(2,1)} copy(bf16[2,8,8192]{2,1,0:T(8,128)(2,1)S(1)} %copy-done.2) | data formatting | bytes 524288 | tf_op args[0]
  68.5 55.3 %gather_fusion = bf16[8192,2,8]{2,1,0:T(2,128)(2,1)} fusion(bf16[2,8,8192]{1,0,2:T(2,128)(2,1)} %copy.73, s32[8192]{0:T(1024)S(1)} %get-tuple-element.54), kind=kCustom, calls=%fused_computation | custom fusion | bytes 557056 | tf_op jit(solution)/shard_map/jit(_take)/gather | solution.py:90
  123.8 9.7 %copy.131 = bf16[2,8,128,64]{3,2,1,0:T(8,128)(2,1)S(1)} copy(bf16[2,8,128,64]{1,0,3,2:T(2,128)(2,1)} %bitcast.332) | data formatting | bytes 524288 | tf_op jit(solution)/shard_map/jit(_take)/gather | solution.py:90
  133.5 0.3 fusion.16
  133.8 0.3 copy.76
  134.1 8.1 %copy.77 = bf16[1,2,64,2,2,2,2,2,2,2,8]{10,9,8,7,6,5,4,3,2,1,0:T(2,128)(2,1)} copy(bf16[1,2,64,2,2,2,2,2,2,2,8]{2,10,3,4,5,6,7,8,9,1,0:T(8,128)(2,1)S(1)} %bitcast.335) | data formatting | bytes 524288 | tf_op jit(solution)/shard_map/transpose | solution.py:36
  142.2 7.0 %reshape.232 = bf16[256,512]{1,0:T(8,128)(2,1)S(1)} reshape(bf16[1,2,64,2,2,2,2,2,2,2,8]{10,9,8,7,6,5,4,3,2,1,0:T(2,128)(2,1)} %copy.77) | data formatting | bytes 524288 | tf_op jit(solution)/shard_map/reshape.14
  149.3 0.3 fusion.8
  149.8 0.3 fusion.9
  150.3 0.3 fusion.10
  150.8 0.4 copy.89
  151.2 0.3 reshape.295
  151.6 0.3 fusion.11
  152.2 0.3 fusion.12
  152.8 0.3 fusion.13
  153.5 0.3 fusion.14
  154.3 3.0 collective-permute-start
  157.6 0.3 convolution_bitcast_fusion.6
  158.0 5.7 %collective-permute-done = bf16[2,64,1024]{2,1,0:T(8,128)(2,1)S(1)} collective-permute-done((bf16[2,64,1024]{2,1,0:T(8,128)(2,1)S(1)}, bf16[2,64,1024]{2,1,0:T(8,128)(2,1)S(1)}, u32[]{:S(2)}, u32[]{:S(2)}) %collective-permute-start) | collective-permute-done | bytes 262176 | tf_op jit(solution)/shard_map/ppermute | solution.py:14
  163.7 0.3 fusion.7
  163.9 1.9 collective-permute-start.1
  165.9 0.3 convolution_bitcast_fusion.4
  166.2 5.3 %collective-permute-done.1 = bf16[2,64,1024]{2,1,0:T(8,128)(2,1)S(1)} collective-permute-done((bf16[2,64,1024]{2,1,0:T(8,128)(2,1)S(1)}, bf16[2,64,1024]{2,1,0:T(8,128)(2,1)S(1)}, u32[]{:S(2)}, u32[]{:S(2)}) %collective-permute-start.1) | collective-permute-done | bytes 262176 | tf_op jit(solution)/shard_map/ppermute | solution.py:14
  171.5 0.3 fusion.6
  171.8 2.5 collective-permute-start.2
  174.4 0.3 convolution_bitcast_fusion.2
  174.7 10.3 %collective-permute-done.2 = bf16[2,64,1024]{2,1,0:T(8,128)(2,1)S(1)} collective-permute-done((bf16[2,64,1024]{2,1,0:T(8,128)(2,1)S(1)}, bf16[2,64,1024]{2,1,0:T(8,128)(2,1)S(1)}, u32[]{:S(2)}, u32[]{:S(2)}) %collective-permute-start.2) | collective-permute-done | bytes 262176 | tf_op jit(solution)/shard_map/ppermute | solution.py:14
  184.9 0.3 fusion.5
  185.2 0.3 copy.103
  185.5 0.3 fusion.15
  185.8 5.5 %copy.149 = bf16[2,8,128,64]{1,0,3,2:T(2,128)(2,1)} copy(bf16[2,8,128,64]{2,3,0,1:T(8,128)(2,1)S(1)} %fusion.15) | data formatting | bytes 524288 | tf_op jit(solution)/shard_map/convert_element_type | solution.py:118
  191.3 6.4 %reshape.326 = bf16[8,2,8192]{2,1,0:T(2,128)(2,1)} reshape(bf16[8192,2,8]{2,1,0:T(2,128)(2,1)} %bitcast.330) | data formatting | bytes 524288
  197.7 5.3 %all-to-all-start = ((bf16[8,2,8192]{2,1,0:T(2,128)(2,1)}), bf16[8,2,8192]{2,1,0:T(2,128)(2,1)S(1)}, u32[]{:S(2)}, u32[]{:S(2)}) async-start(bf16[8,2,8192]{2,1,0:T(2,128)(2,1)} %reshape.326), calls=%async_computation | async-start | bytes 524288 | tf_op jit(solution)/shard_map/all_to_all | solution.py:117
  203.0 30.5 %scatter_custom_fusion = s32[8192]{0:T(1024)S(1)} fusion(s32[8192]{0:T(1024)S(1)} %get-tuple-element.53, s32[8192]{0:T(1024)S(1)} %iota.3, s32[]{:T(128)} %constant.32.clone.1), kind=kCustom, calls=%fused_computation.167 | custom fusion | bytes 32772 | tf_op jit(solution)/shard_map/scatter | solution.py:125
  233.5 6.2 %reshape.327 = bf16[8192,2,8]{2,1,0:T(2,128)(2,1)} reshape(bf16[8,2,8192]{2,1,0:T(2,128)(2,1)S(1)} %all-to-all-done) | data formatting | bytes 524288
  239.7 9.4 %convert_bitcast_fusion = f32[2,8,16,2,2,2,64]{1,0,6,2,3,4,5:T(2,128)} fusion(bf16[2,8,2,2,2,16,64]{1,0,6,5,4,3,2:T(2,128)(2,1)} %bitcast.329), kind=kLoop, calls=%fused_computation.4 | loop fusion | flops 131072 | bytes 786432 | tf_op jit(solution)/shard_map/reshape | solution.py:121
  249.1 7.4 %copy.150 = f32[2,8,16,2,2,2,64]{1,0,6,5,4,3,2:T(2,128)} copy(f32[2,8,16,2,2,2,64]{1,0,6,2,3,4,5:T(2,128)} %convert_bitcast_fusion) | data formatting | bytes 1048576 | tf_op jit(solution)/shard_map/reshape | solution.py:121
  256.5 59.5 %gather_fusion.2 = f32[8192,2,8]{2,1,0:T(2,128)} fusion(f32[2,8,8192]{1,0,2:T(2,128)} %bitcast.331, s32[8192]{0:T(1024)S(1)} %fusion.76), kind=kCustom, calls=%fused_computation.2 | custom fusion | bytes 1081344 | tf_op jit(solution)/shard_map/jit(_take)/gather | solution.py:127
  316.0 30.9 %select_bitcast_fusion = f32[2,8,8192]{1,0,2:T(2,128)} fusion(f32[8192,2,8]{2,1,0:T(2,128)} %gather_fusion.2, pred[8192]{0:T(1024)(128)(4,1)S(1)} %compare_and_fusion.1), kind=kLoop, calls=%fused_computation.5 | loop fusion | flops 131072 | bytes 1056768 | tf_op jit(solution)/shard_map/jit(_take)/select_n | solution.py:127
  346.9 10.0 %copy.109 = f32[2,8,8192]{2,1,0:T(8,128)} copy(f32[2,8,8192]{1,0,2:T(2,128)} %select_bitcast_fusion) | data formatting | bytes 1048576 | tf_op jit(solution)/shard_map/jit(_take)/select_n | solution.py:127
  (52 shorter events, 4.3 us)
Async XLA Ops:
  0.0 6.3 %copy-start = (f32[8192]{0:T(1024)S(1)}, f32[8192]{0:T(1024)}, u32[]{:S(2)}) copy-start(f32[8192]{0:T(1024)} %param.7) | copy-start | bytes 98308
  6.3 45.6 %copy-start.3 = (s32[8192]{0:T(1024)S(1)}, s32[8192]{0:T(1024)}, u32[]{:S(2)}) copy-start(s32[8192]{0:T(1024)} %param.8) | copy-start | bytes 98308
  55.6 6.1 %copy-start.2 = (bf16[2,8,8192]{2,1,0:T(8,128)(2,1)S(1)}, bf16[2,8,8192]{2,1,0:T(8,128)(2,1)}, u32[]{:S(2)}) copy-start(bf16[2,8,8192]{2,1,0:T(8,128)(2,1)} %param.6) | copy-start | bytes 786436
  151.6 5.8 %copy-start.4 = (bf16[2,64,64]{2,1,0:T(8,128)(2,1)S(1)}, bf16[2,64,64]{2,1,0:T(8,128)(2,1)}, u32[]{:S(2)}) copy-start(bf16[2,64,64]{2,1,0:T(8,128)(2,1)} %param.11) | copy-start | bytes 49156
  154.3 9.3 %collective-permute-start = (bf16[2,64,1024]{2,1,0:T(8,128)(2,1)S(1)}, bf16[2,64,1024]{2,1,0:T(8,128)(2,1)S(1)}, u32[]{:S(2)}, u32[]{:S(2)}) collective-permute-start(bf16[2,64,1024]{2,1,0:T(8,128)(2,1)S(1)} %copy.102), channel_id=1, source_target_pairs={{0,4},{4,0},{8,12},{12,8},{16,20},{20,16},{24,28},{28,24},{1,5},{5... | collective-permute-start | bytes 786440 | tf_op jit(solution)/shard_map/ppermute | solution.py:14
  163.9 7.6 %collective-permute-start.1 = (bf16[2,64,1024]{2,1,0:T(8,128)(2,1)S(1)}, bf16[2,64,1024]{2,1,0:T(8,128)(2,1)S(1)}, u32[]{:S(2)}, u32[]{:S(2)}) collective-permute-start(bf16[2,64,1024]{2,1,0:T(8,128)(2,1)S(1)} %fusion.7), channel_id=1, source_target_pairs={{0,8},{8,0},{4,12},{12,4},{16,24},{24,16},{20,28},{28,20},{1,9},{9... | collective-permute-start | bytes 786440 | tf_op jit(solution)/shard_map/ppermute | solution.py:14
  171.8 13.2 %collective-permute-start.2 = (bf16[2,64,1024]{2,1,0:T(8,128)(2,1)S(1)}, bf16[2,64,1024]{2,1,0:T(8,128)(2,1)S(1)}, u32[]{:S(2)}, u32[]{:S(2)}) collective-permute-start(bf16[2,64,1024]{2,1,0:T(8,128)(2,1)S(1)} %fusion.6), channel_id=1, source_target_pairs={{0,16},{16,0},{4,20},{20,4},{8,24},{24,8},{12,28},{28,12},{1,17},{... | collective-permute-start | bytes 786440 | tf_op jit(solution)/shard_map/ppermute | solution.py:14
  197.7 35.8 %all-to-all-start = ((bf16[8,2,8192]{2,1,0:T(2,128)(2,1)}), bf16[8,2,8192]{2,1,0:T(2,128)(2,1)S(1)}, u32[]{:S(2)}, u32[]{:S(2)}) async-start(bf16[8,2,8192]{2,1,0:T(2,128)(2,1)} %reshape.326), calls=%async_computation | async-start | bytes 524288 | tf_op jit(solution)/shard_map/all_to_all | solution.py:117
  316.0 40.8 %copy-start.1 = (f32[8192]{0:T(1024)S(1)}, f32[8192]{0:T(1024)}, u32[]{:S(2)}) copy-start(f32[8192]{0:T(1024)} %param.7) | copy-start | bytes 98308
where the time goes:
time: 358 us; the launch traced here: 357 us
  local copies, waits for them, and re-layouts  269 us (75%)
  other arithmetic  49.2 us (14%)
  waiting for transfers between devices  21.2 us (6%)
  starting transfers between devices  12.7 us (4%)
  matrix products  4.12 us (1%)
    gather x2, local copies, waits for them, and re-layouts, per_device(): in_tree = jnp.take(excitation, tree_order, axis=2)  65 us
    gather x1, local copies, waits for them, and re-layouts, per_device(): out_field = jnp.take(potential, inverse, axis=2)  59.5 us
    gather x1, local copies, waits for them, and re-layouts, per_device(): weights_tree = jnp.take(source_weight, tree_order)  45.5 us
    select_n x1, other arithmetic, per_device(): out_field = jnp.take(potential, inverse, axis=2)  30.9 us
    scatter x1, local copies, waits for them, and re-layouts, per_device(): inverse = jnp.zeros((point_count,), jnp.int32).at[tree_order].set(jnp.ara...  30.5 us
    ppermute x3, waiting for transfers between devices, swapped(): return lax.ppermute(block, axis, route)  21.2 us
    unnamed x13, local copies, waits for them, and re-layouts  19.4 us
    select_n x1, local copies, waits for them, and re-layouts, per_device(): out_field = jnp.take(potential, inverse, axis=2)  9.95 us
  transfers between devices with their start and end apart: 4, of which 3 were waited for; matrix products, arithmetic and copies ran while one was open for 9% of the time, Pallas kernels for 0%

commit v1 on v0

v1 whole, which is shorter than its diff:
```python
import functools
import jax
import jax.numpy as jnp
from jax import lax
from jax.experimental import pallas as pl
from jax.experimental.pallas import tpu as pltpu
from jax.sharding import PartitionSpec as P

LANES = 256
VMEM_BYTES = 48 * 1024 * 1024


def dot_rows(left, right):
    return lax.dot_general(
        left, right, (((1,), (1,)), ((), ())), preferred_element_type=jnp.float32
    )


def level_matrix(transfer_ref, level):
    rank = transfer_ref.shape[3]
    rows = []
    for child in range(2):
        real = transfer_ref[level, 0, child]
        imag = transfer_ref[level, 1, child]
        real_0, real_1 = real[:, :rank], real[:, rank:]
        imag_0, imag_1 = imag[:, :rank], imag[:, rank:]
        rows.append(jnp.concatenate([real_0, -imag_0, real_1, -imag_1], axis=1))
        rows.append(jnp.concatenate([imag_0, real_0, imag_1, real_1], axis=1))
    return jnp.concatenate(rows, axis=0)


def leaf_matrix(basis_ref):
    real, imag = basis_ref[0], basis_ref[1]
    zero = jnp.zeros_like(real)
    rows = [
        jnp.concatenate([real, zero, -imag, zero], axis=1),
        jnp.concatenate([imag, zero, real, zero], axis=1),
        jnp.concatenate([zero, real, zero, -imag], axis=1),
        jnp.concatenate([zero, imag, zero, real], axis=1),
    ]
    return jnp.concatenate(rows, axis=0)


def eval_matrix(basis_ref):
    real, imag = basis_ref[0], basis_ref[1]
    zero = jnp.zeros_like(real)
    rows = [
        jnp.concatenate([real, -imag, zero, zero], axis=1),
        jnp.concatenate([zero, zero, real, -imag], axis=1),
        jnp.concatenate([imag, real, zero, zero], axis=1),
        jnp.concatenate([zero, zero, imag, real], axis=1),
    ]
    return jnp.concatenate(rows, axis=0)


def pair_up(state, targets, vecs):
    rows, width = state.shape
    block = targets * vecs
    if block % 16:
        state = state.astype(jnp.float32)
    split = state.reshape(rows // (2 * block), 2, block, width)
    joined = jnp.concatenate([split[:, 0], split[:, 1]], axis=-1)
    return joined.reshape(rows // 2, 2 * width).astype(jnp.bfloat16)


def children(result, vecs):
    rows, width = result.shape
    half = width // 2
    blocks = result.reshape(rows // vecs, vecs, width)
    stacked = jnp.stack([blocks[..., :half], blocks[..., half:]], axis=1)
    return stacked.reshape(rows * 2, half).astype(jnp.bfloat16)


def one_hot(order_block):
    low = jnp.bitwise_and(order_block, LANES - 1)
    rows = lax.broadcasted_iota(jnp.int32, (LANES, order_block.shape[1]), 0)
    return jnp.where(rows == low, 1.0, 0.0).astype(jnp.bfloat16)


def near_kernel(local_levels, exc_ref, weight_ref, order_ref, leaf_ref, transfer_ref,
                out_ref, weighted, pairs):
    vecs = exc_ref.shape[1]
    points = exc_ref.shape[2]
    blocks = points // LANES
    half = LANES // 2
    for block in range(blocks):
        lanes = pl.ds(block * LANES, LANES)
        scaled = [
            exc_ref[part, :, lanes].astype(jnp.float32) * weight_ref[:, lanes] for part in range(2)
        ]
        weighted[pl.ds(block * 2 * vecs, 2 * vecs), :] = jnp.concatenate(scaled, axis=0).astype(
            jnp.bfloat16
        )

    def gather(step, carry):
        order = order_ref[:, pl.ds(pl.multiple_of(step * LANES, LANES), LANES)]
        spread = jnp.dot(weighted[...], one_hot(order), preferred_element_type=jnp.float32)
        high = jnp.broadcast_to(lax.shift_right_logical(order, 8), (2 * vecs, LANES))
        picked = spread[: 2 * vecs]
        for block in range(1, blocks):
            picked = jnp.where(
                high == block, spread[block * 2 * vecs : (block + 1) * 2 * vecs], picked
            )
        rows = [
            jnp.concatenate([picked[:vecs, lo : lo + half], picked[vecs:, lo : lo + half]], axis=1)
            for lo in (0, half)
        ]
        pairs[pl.ds(pl.multiple_of(step * 2 * vecs, 2 * vecs), 2 * vecs), :] = jnp.concatenate(
            rows, axis=0
        ).astype(jnp.bfloat16)
        return carry

    lax.fori_loop(0, blocks, gather, 0, unroll=2)
    joined = dot_rows(pairs[...], leaf_matrix(leaf_ref)).astype(jnp.bfloat16)
    for level in range(local_levels):
        result = dot_rows(joined, level_matrix(transfer_ref, level))
        state = children(result, vecs)
        if level + 1 < local_levels:
            joined = pair_up(state, 2 << level, vecs)
    out_ref[...] = state


def far_kernel(local_levels, per_peer, vecs, state_ref, order_ref, transfer_ref, eval_ref,
               out_ref, values, total):
    levels = transfer_ref.shape[0]
    points = order_ref.shape[1]
    blocks = points // LANES
    half = LANES // 2
    state = state_ref[...]
    targets = per_peer
    for level in range(local_levels, levels):
        result = dot_rows(pair_up(state, targets, vecs), level_matrix(transfer_ref, level))
        state = children(result, vecs)
        targets *= 2
    joined = pair_up(state, 1, vecs)
    values[...] = dot_rows(joined, eval_matrix(eval_ref))
    total[...] = jnp.zeros_like(total)

    def scatter(step, carry):
        order = order_ref[:, pl.ds(pl.multiple_of(step * LANES, LANES), LANES)]
        held = values[pl.ds(pl.multiple_of(step * 2 * vecs, 2 * vecs), 2 * vecs), :]
        block_values = jnp.concatenate(
            [
                jnp.concatenate([held[:vecs, lo : lo + half], held[vecs:, lo : lo + half]], axis=1)
                for lo in (0, half)
            ],
            axis=0,
        )
        high = jnp.broadcast_to(lax.shift_right_logical(order, 8), (2 * vecs, LANES))
        spread = jnp.concatenate(
            [jnp.where(high == block, block_values, 0.0).astype(jnp.bfloat16) for block in range(blocks)],
            axis=0,
        )
        total[...] += dot_rows(spread, one_hot(order))
        return carry

    lax.fori_loop(0, blocks, scatter, 0, unroll=2)
    for block in range(blocks):
        rows = block * 2 * vecs
        for part in range(2):
            out_ref[part, :, pl.ds(block * LANES, LANES)] = total[
                pl.ds(rows + part * vecs, vecs), :
            ]


def per_device(excitation, source_weight, tree_order, leaf_basis, transfer, eval_basis):
    vecs, points = excitation.shape[1:]
    levels, rank = transfer.shape[0], leaf_basis.shape[1]
    leaf_size = leaf_basis.shape[2]
    boxes = points // leaf_size
    count = lax.axis_size("leaf")
    cross_levels = count.bit_length() - 1
    local_levels = levels - cross_levels
    per_peer = boxes // count
    transfer = transfer.reshape(levels, 2, 2, rank, 2 * rank)
    weight_row = source_weight.reshape(1, points)
    order_row = tree_order.reshape(1, points)
    params = pltpu.CompilerParams(vmem_limit_bytes=VMEM_BYTES)
    wide = points // LANES * 2 * vecs
    state = pl.pallas_call(
        functools.partial(near_kernel, local_levels),
        out_shape=jax.ShapeDtypeStruct((boxes * vecs, 2 * rank), jnp.bfloat16),
        scratch_shapes=[
            pltpu.VMEM((wide, LANES), jnp.bfloat16),
            pltpu.VMEM((boxes * vecs // 2, 4 * rank), jnp.bfloat16),
        ],
        compiler_params=params,
        name="near",
    )(excitation, weight_row, order_row, leaf_basis, transfer)
    state = lax.all_to_all(state, "leaf", split_axis=0, concat_axis=0, tiled=True)
    return pl.pallas_call(
        functools.partial(far_kernel, local_levels, per_peer, vecs),
        out_shape=jax.ShapeDtypeStruct((2, vecs, points), jnp.float32),
        scratch_shapes=[
            pltpu.VMEM((boxes * vecs // 2, 4 * rank), jnp.float32),
            pltpu.VMEM((wide, LANES), jnp.float32),
        ],
        compiler_params=params,
        name="far",
    )(state, order_row, transfer, eval_basis)


def solution(mesh):
    in_specs = (P(None, "rhs", "leaf"), P("leaf"), P("leaf"), P(), P(), P())
    return jax.shard_map(
        per_device, mesh=mesh, in_specs=in_specs, out_specs=P(None, "rhs", "leaf"), check_vma=False
    )
```

time: 358 us -> 32.6 us (0.09)
  local copies, waits for them, and re-layouts: 269 us -> 2.77 us
  other arithmetic: 49.2 us -> 0 us
  waiting for transfers between devices: 21.2 us -> 0 us
  blocking collectives: 0 us -> 16 us
  Pallas kernels: 0 us -> 13.6 us
  starting transfers between devices: 12.7 us -> 0 us
  matrix products: 4.12 us -> 0 us
    gather x4 -> x0, local copies, waits for them, and re-layouts: 170 us -> none  [the longest x2 65 us: per_device(): in_tree = jnp.take(excitation, tree_order, axis=2)]
    select_n x6 -> x0, other arithmetic: 31.8 us -> none  [the longest x1 30.9 us: per_device(): out_field = jnp.take(potential, inverse, axis=2)]
    scatter x1 -> x0, local copies, waits for them, and re-layouts: 30.5 us -> none  [per_device(): inverse = jnp.zeros((point_count,), jnp.int32).at[tree_order].set(jnp.ara...]
    ppermute x3 -> x0, waiting for transfers between devices: 21.2 us -> none  [swapped(): return lax.ppermute(block, axis, route)]
    unnamed x13 -> x10, local copies, waits for them, and re-layouts: 19.4 us -> 0.02 us
    all_to_all x0 -> x1, blocking collectives: none -> 16 us  [per_device(): lax.all_to_all(state, 'leaf', split_axis=0, concat_axis=0, tiled=True)]
    pallas_call x0 -> x2, Pallas kernels: none -> 13.6 us  [the longest x1 7.38 us: per_device(): pl.pallas_call(functools.partial(far_kernel, local_levels, per_peer, vecs...]
    transpose x9 -> x0, local copies, waits for them, and re-layouts: 11.1 us -> none  [the longest x1 8.09 us: run_levels(): jnp.transpose(split_bits, order)]
  transfers between devices with their start and end apart: 4 -> 0, of which waited for: 3 -> 0; matrix products, arithmetic and copies ran while one was open for 9% -> 0% of each run, Pallas kernels for 0% -> 0%
where the time goes in v1:
time: 32.6 us; the launch traced here: 32.4 us
  blocking collectives  16 us (49%)
  Pallas kernels  13.6 us (42%)
  local copies, waits for them, and re-layouts  2.77 us (8%)
    all_to_all x1, blocking collectives, per_device(): lax.all_to_all(state, 'leaf', split_axis=0, concat_axis=0, tiled=True)  16 us
    pallas_call x1, Pallas kernels, per_device(): pl.pallas_call(functools.partial(far_kernel, local_levels, per_peer, vecs...  7.38 us
    pallas_call x1, Pallas kernels, per_device(): pl.pallas_call(functools.partial(near_kernel, local_levels), out_shape=ja...  6.19 us
    reshape x1, local copies, waits for them, and re-layouts, per_device(): transfer = transfer.reshape(levels, 2, 2, rank, 2 * rank)  2.75 us

profile of v1, /device:TPU:0, one launch (start us, length us, event | category | flops | bytes accessed | tf_op | source)
XLA Modules:
  0.0 32.4 jit_solution(10392566071321439346)
XLA Ops:
  0.0 0.0 copy-start.3
  0.0 0.0 copy-start.1
  0.0 0.0 copy-start.2
  0.0 0.0 copy-start
  0.0 2.7 %reshape.13.transfer_ref = bf16[10,2,2,64,128]{4,3,2,1,0:T(8,128)(2,1)S(1)} reshape(bf16[10,2,2,64,2,64]{5,4,3,2,1,0:T(2,128)(2,1)} %param.10) | data formatting | bytes 1310720 | tf_op jit(solution)/shard_map/reshape | solution.py:175
  2.8 0.0 copy-start.4
  2.8 0.0 copy-done.3
  2.8 0.0 copy-done.1
  2.8 0.0 copy-done.2
  2.8 0.0 copy-done
  2.8 6.2 %near.1 = bf16[1024,128]{1,0:T(8,128)(2,1)S(1)} custom-call(bf16[2,8,8192]{2,1,0:T(8,128)(2,1)S(1)} %copy-done, f32[1,8192]{1,0:T(1,128)S(1)} %bitcast.8, s32[1,8192]{1,0:T(1,128)S(1)} %bitcast.6, bf16[2,64,64]{2,1,0:T(8,128)(2,1)S(1)} %copy-done.3, bf16[10,2,2,64,128]{4,3,2,1,0:T(8,128)(2,1)S(1)} %reshape.13.transfer_ref), custom_call_target="tpu_custom_call" | custom-call | tf_op jit(solution)/shard_map/near/pallas_call | solution.py:180
  9.0 16.0 %all_to_all.11 = bf16[8,128,128]{2,1,0:T(8,128)(2,1)S(1)} all-to-all(bf16[8,128,128]{2,1,0:T(8,128)(2,1)S(1)} %bitcast.4), channel_id=1, replica_groups=mesh['leaf'=8,'rhs'=4] {'leaf'}, dimensions={0} | all-to-all | bytes 524288 | tf_op jit(solution)/shard_map/all_to_all | solution.py:190
  25.0 0.0 copy-done.4
  25.0 7.4 %far.1 = f32[2,8,8192]{2,1,0:T(8,128)} custom-call(bf16[1024,128]{1,0:T(8,128)(2,1)S(1)} %bitcast.5, s32[1,8192]{1,0:T(1,128)S(1)} %bitcast.7, bf16[10,2,2,64,128]{4,3,2,1,0:T(8,128)(2,1)S(1)} %reshape.13.transfer_ref, bf16[2,64,64]{2,1,0:T(8,128)(2,1)S(1)} %copy-done.4), custom_call_target="tpu_custom_call" | custom-call | tf_op jit(solution)/shard_map/far/pallas_call | solution.py:191
Async XLA Ops:
  0.0 2.8 %copy-start.3 = (bf16[2,64,64]{2,1,0:T(8,128)(2,1)S(1)}, bf16[2,64,64]{2,1,0:T(8,128)(2,1)}, u32[]{:S(2)}) copy-start(bf16[2,64,64]{2,1,0:T(8,128)(2,1)} %leaf_ref.1) | copy-start | bytes 49156
  0.0 2.8 %copy-start.1 = (s32[8192]{0:T(1024)S(1)}, s32[8192]{0:T(1024)}, u32[]{:S(2)}) copy-start(s32[8192]{0:T(1024)} %param.8) | copy-start | bytes 98308
  0.0 2.8 %copy-start.2 = (f32[8192]{0:T(1024)S(1)}, f32[8192]{0:T(1024)}, u32[]{:S(2)}) copy-start(f32[8192]{0:T(1024)} %param.7) | copy-start | bytes 98308
  0.0 2.8 %copy-start = (bf16[2,8,8192]{2,1,0:T(8,128)(2,1)S(1)}, bf16[2,8,8192]{2,1,0:T(8,128)(2,1)}, u32[]{:S(2)}) copy-start(bf16[2,8,8192]{2,1,0:T(8,128)(2,1)} %exc_ref.1) | copy-start | bytes 786436
  2.8 22.3 %copy-start.4 = (bf16[2,64,64]{2,1,0:T(8,128)(2,1)S(1)}, bf16[2,64,64]{2,1,0:T(8,128)(2,1)}, u32[]{:S(2)}) copy-start(bf16[2,64,64]{2,1,0:T(8,128)(2,1)} %eval_ref.1) | copy-start | bytes 49156

commit v2 on v1

v2 whole, which is shorter than its diff:
```python
import functools
import jax
import jax.numpy as jnp
from jax import lax
from jax.experimental import pallas as pl
from jax.experimental.pallas import tpu as pltpu
from jax.sharding import PartitionSpec as P

LANES = 256
CHUNKS = 2
VMEM_BYTES = 56 * 1024 * 1024


def dot_rows(left, right):
    return lax.dot_general(
        left, right, (((1,), (1,)), ((), ())), preferred_element_type=jnp.float32
    )


def level_matrix(transfer_ref, level, halves):
    rank = transfer_ref.shape[4]
    for part in range(2):
        for child in range(2):
            halves[part, child] = transfer_ref[level, part, child].astype(jnp.float32)
    rows = []
    for child in range(2):
        real_0, real_1 = (halves[0, child, pl.ds(half, rank, stride=2), :] for half in range(2))
        imag_0, imag_1 = (halves[1, child, pl.ds(half, rank, stride=2), :] for half in range(2))
        rows.append(jnp.concatenate([real_0, -imag_0, real_1, -imag_1], axis=1))
        rows.append(jnp.concatenate([imag_0, real_0, imag_1, real_1], axis=1))
    return jnp.concatenate(rows, axis=0).astype(jnp.bfloat16)


def leaf_matrix(basis_ref):
    real, imag = basis_ref[0], basis_ref[1]
    zero = jnp.zeros_like(real)
    rows = [
        jnp.concatenate([real, zero, -imag, zero], axis=1),
        jnp.concatenate([imag, zero, real, zero], axis=1),
        jnp.concatenate([zero, real, zero, -imag], axis=1),
        jnp.concatenate([zero, imag, zero, real], axis=1),
    ]
    return jnp.concatenate(rows, axis=0)


def eval_matrix(basis_ref):
    real, imag = basis_ref[0], basis_ref[1]
    zero = jnp.zeros_like(real)
    rows = [
        jnp.concatenate([real, -imag, zero, zero], axis=1),
        jnp.concatenate([zero, zero, real, -imag], axis=1),
        jnp.concatenate([imag, real, zero, zero], axis=1),
        jnp.concatenate([zero, zero, imag, real], axis=1),
    ]
    return jnp.concatenate(rows, axis=0)


def pair_up(state, targets, vecs):
    rows, width = state.shape
    block = targets * vecs
    if block % 16:
        state = state.astype(jnp.float32)
    split = state.reshape(rows // (2 * block), 2, block, width)
    joined = jnp.concatenate([split[:, 0], split[:, 1]], axis=-1)
    return joined.reshape(rows // 2, 2 * width).astype(jnp.bfloat16)


def children(result, vecs):
    rows, width = result.shape
    half = width // 2
    blocks = result.reshape(rows // vecs, vecs, width)
    stacked = jnp.stack([blocks[..., :half], blocks[..., half:]], axis=1)
    return stacked.reshape(rows * 2, half).astype(jnp.bfloat16)


def one_hot(order_block):
    low = jnp.bitwise_and(order_block, LANES - 1)
    rows = lax.broadcasted_iota(jnp.int32, (LANES, order_block.shape[1]), 0)
    return jnp.where(rows == low, 1.0, 0.0).astype(jnp.bfloat16)


def aligned(index, size):
    return pl.ds(pl.multiple_of(index * size, size), size)


def weigh(exc_ref, weight_ref, weighted):
    vecs, points = exc_ref.shape[1:]
    for block in range(points // LANES):
        lanes = pl.ds(block * LANES, LANES)
        scaled = [
            exc_ref[part, :, lanes].astype(jnp.float32) * weight_ref[:, lanes] for part in range(2)
        ]
        weighted[pl.ds(block * 2 * vecs, 2 * vecs), :] = jnp.concatenate(scaled, axis=0).astype(
            jnp.bfloat16
        )


def gather_step(step, vecs, blocks, order_ref, weighted, hot, pairs):
    half = LANES // 2
    order = order_ref[:, aligned(step, LANES)]
    table = one_hot(order)
    hot[step] = table
    spread = jnp.dot(weighted[...], table, preferred_element_type=jnp.float32)
    high = jnp.broadcast_to(lax.shift_right_logical(order, 8), (vecs, LANES))
    real, imag = spread[:vecs], spread[vecs : 2 * vecs]
    for block in range(1, blocks):
        here = high == block
        base = block * 2 * vecs
        real = jnp.where(here, spread[base : base + vecs], real)
        imag = jnp.where(here, spread[base + vecs : base + 2 * vecs], imag)
    rows = [
        jnp.concatenate([real[:, lo : lo + half], imag[:, lo : lo + half]], axis=1)
        for lo in (0, half)
    ]
    pairs[aligned(step, 2 * vecs), :] = jnp.concatenate(rows, axis=0).astype(jnp.bfloat16)


def scatter_steps(group, vecs, blocks, count, order_ref, hot, values, total):
    half = LANES // 2
    spreads, tables = [], []
    for inner in range(count):
        step = group * count + inner
        order = order_ref[:, aligned(step, LANES)]
        held = values[aligned(step, 2 * vecs), :]
        real, imag = (
            jnp.concatenate([held[:vecs, lo : lo + half], held[vecs:, lo : lo + half]], axis=1)
            for lo in (0, half)
        )
        high = jnp.broadcast_to(lax.shift_right_logical(order, 8), (vecs, LANES))
        rows = []
        for block in range(blocks):
            here = high == block
            rows.append(jnp.where(here, real, 0.0))
            rows.append(jnp.where(here, imag, 0.0))
        spreads.append(jnp.concatenate(rows, axis=0).astype(jnp.bfloat16))
        tables.append(hot[step])
    total[...] += dot_rows(jnp.concatenate(spreads, axis=1), jnp.concatenate(tables, axis=1))


def write_out(vecs, blocks, total, out_ref):
    for block in range(blocks):
        rows = block * 2 * vecs
        for part in range(2):
            out_ref[part, :, pl.ds(block * LANES, LANES)] = total[
                pl.ds(rows + part * vecs, vecs), :
            ]


def fused_kernel(count, chunks, near_levels, exc_ref, weight_ref, order_ref, leaf_ref, transfer_ref,
                 eval_ref, out_ref, weighted, pairs, hot, mats, halves, sent, held, values, total,
                 send_sems, recv_sems):
    vecs, points = exc_ref.shape[1:]
    levels = transfer_ref.shape[0]
    blocks = points // LANES
    me = lax.axis_index("leaf")
    peers = [(hop, lax.rem(me + hop, count)) for hop in range(1, count)]
    barrier = pltpu.get_barrier_semaphore()
    for hop, peer in peers:
        pl.semaphore_signal(
            barrier, inc=1, device_id={"leaf": peer}, device_id_type=pl.DeviceIdType.MESH
        )
    weigh(exc_ref, weight_ref, weighted)
    for level in range(near_levels):
        mats[level] = level_matrix(transfer_ref, level, halves)
    mats[levels] = leaf_matrix(leaf_ref)
    steps = blocks // chunks
    rows = sent.shape[2]
    copies = []
    for chunk in range(chunks):

        def gather(step, carry):
            gather_step(chunk * steps + step, vecs, blocks, order_ref, weighted, hot, pairs)
            return carry

        lax.fori_loop(0, steps, gather, 0, unroll=2)
        start = chunk * steps * 2 * vecs
        joined = dot_rows(pairs[start : start + steps * 2 * vecs, :], mats[levels]).astype(
            jnp.bfloat16
        )
        for level in range(near_levels):
            state = children(dot_rows(joined, mats[level]), vecs)
            if level + 1 < near_levels:
                joined = pair_up(state, 2 << level, vecs)
        sent[chunk] = state.reshape(count, rows, state.shape[1])
        if chunk == 0:
            pl.semaphore_wait(barrier, count - 1)
        for hop, peer in peers:
            copy = pltpu.make_async_remote_copy(
                src_ref=sent.at[chunk, peer],
                dst_ref=held.at[me * chunks + chunk],
                send_sem=send_sems.at[chunk, hop],
                recv_sem=recv_sems.at[chunk, hop],
                device_id={"leaf": peer},
                device_id_type=pl.DeviceIdType.MESH,
            )
            copy.start()
            copies.append(copy)
        held[me * chunks + chunk] = sent[chunk, me]
    for level in range(near_levels, levels):
        mats[level] = level_matrix(transfer_ref, level, halves)
    mats[levels + 1] = eval_matrix(eval_ref)
    total[...] = jnp.zeros_like(total)
    for copy in copies:
        copy.wait()
    state = held[...].reshape(count * chunks * rows, held.shape[2])
    targets = rows // vecs
    for level in range(near_levels, levels):
        state = children(dot_rows(pair_up(state, targets, vecs), mats[level]), vecs)
        targets *= 2
    values[...] = dot_rows(pair_up(state, 1, vecs), mats[levels + 1])
    group = 2

    def scatter(step, carry):
        scatter_steps(step, vecs, blocks, group, order_ref, hot, values, total)
        return carry

    lax.fori_loop(0, blocks // group, scatter, 0)
    write_out(vecs, blocks, total, out_ref)


def near_kernel(near_levels, exc_ref, weight_ref, order_ref, leaf_ref, transfer_ref,
                out_ref, weighted, hot, pairs, halves):
    vecs, points = exc_ref.shape[1:]
    blocks = points // LANES
    weigh(exc_ref, weight_ref, weighted)

    def gather(step, carry):
        gather_step(step, vecs, blocks, order_ref, weighted, hot, pairs)
        return carry

    lax.fori_loop(0, blocks, gather, 0)
    joined = dot_rows(pairs[...], leaf_matrix(leaf_ref)).astype(jnp.bfloat16)
    for level in range(near_levels):
        state = children(dot_rows(joined, level_matrix(transfer_ref, level, halves)), vecs)
        if level + 1 < near_levels:
            joined = pair_up(state, 2 << level, vecs)
    out_ref[...] = state


def far_kernel(near_levels, per_peer, vecs, state_ref, order_ref, transfer_ref, eval_ref,
               out_ref, hot, values, total, halves):
    blocks = order_ref.shape[1] // LANES
    state = state_ref[...]
    targets = per_peer
    for level in range(near_levels, transfer_ref.shape[0]):
        matrix = level_matrix(transfer_ref, level, halves)
        state = children(dot_rows(pair_up(state, targets, vecs), matrix), vecs)
        targets *= 2
    values[...] = dot_rows(pair_up(state, 1, vecs), eval_matrix(eval_ref))
    total[...] = jnp.zeros_like(total)

    def scatter(step, carry):
        hot[step] = one_hot(order_ref[:, aligned(step, LANES)])
        scatter_steps(step, vecs, blocks, 1, order_ref, hot, values, total)
        return carry

    lax.fori_loop(0, blocks, scatter, 0)
    write_out(vecs, blocks, total, out_ref)


def per_device(excitation, source_weight, tree_order, leaf_basis, transfer, eval_basis):
    vecs, points = excitation.shape[1:]
    levels, rank = transfer.shape[0], leaf_basis.shape[1]
    leaf_size = leaf_basis.shape[2]
    boxes = points // leaf_size
    blocks = points // LANES
    count = lax.axis_size("leaf")
    transfer = transfer.reshape(levels, 2, 2, 2 * rank, rank)
    weight_row = source_weight.reshape(1, points)
    order_row = tree_order.reshape(1, points)
    box_levels = boxes.bit_length() - 1
    out_shape = jax.ShapeDtypeStruct((2, vecs, points), jnp.float32)
    weighted = pltpu.VMEM((blocks * 2 * vecs, LANES), jnp.bfloat16)
    pairs = pltpu.VMEM((boxes * vecs // 2, 4 * rank), jnp.bfloat16)
    values = pltpu.VMEM((boxes * vecs // 2, 4 * rank), jnp.float32)
    total = pltpu.VMEM((blocks * 2 * vecs, LANES), jnp.float32)
    hot = pltpu.VMEM((blocks, LANES, LANES), jnp.bfloat16)
    halves = pltpu.VMEM((2, 2, 2 * rank, rank), jnp.float32)
    chunks = CHUNKS
    while chunks > 1 and boxes // chunks // count * vecs < 16:
        chunks //= 2
    rows = boxes // chunks // count * vecs
    if rows >= 16:
        near_levels = box_levels - (chunks.bit_length() - 1)
        return pl.pallas_call(
            functools.partial(fused_kernel, count, chunks, near_levels),
            out_shape=out_shape,
            in_specs=[pl.BlockSpec(memory_space=pltpu.VMEM)] * 6,
            out_specs=pl.BlockSpec(memory_space=pltpu.VMEM),
            scratch_shapes=[
                weighted,
                pairs,
                hot,
                pltpu.VMEM((levels + 2, 4 * rank, 4 * rank), jnp.bfloat16),
                halves,
                pltpu.VMEM((chunks, count, rows, 2 * rank), jnp.bfloat16),
                pltpu.VMEM((count * chunks, rows, 2 * rank), jnp.bfloat16),
                values,
                total,
                pltpu.SemaphoreType.DMA((chunks, count)),
                pltpu.SemaphoreType.DMA((chunks, count)),
            ],
            compiler_params=pltpu.CompilerParams(
                vmem_limit_bytes=VMEM_BYTES, collective_id=0, has_side_effects=True
            ),
            name="fused",
        )(excitation, weight_row, order_row, leaf_basis, transfer, eval_basis)
    params = pltpu.CompilerParams(vmem_limit_bytes=VMEM_BYTES)
    state = pl.pallas_call(
        functools.partial(near_kernel, box_levels),
        out_shape=jax.ShapeDtypeStruct((boxes * vecs, 2 * rank), jnp.bfloat16),
        scratch_shapes=[weighted, hot, pairs, halves],
        compiler_params=params,
        name="near",
    )(excitation, weight_row, order_row, leaf_basis, transfer)
    state = lax.all_to_all(state, "leaf", split_axis=0, concat_axis=0, tiled=True)
    return pl.pallas_call(
        functools.partial(far_kernel, box_levels, boxes // count, vecs),
        out_shape=out_shape,
        scratch_shapes=[hot, values, total, halves],
        compiler_params=params,
        name="far",
    )(state, order_row, transfer, eval_basis)


def solution(mesh):
    in_specs = (P(None, "rhs", "leaf"), P("leaf"), P("leaf"), P(), P(), P())
    return jax.shard_map(
        per_device, mesh=mesh, in_specs=in_specs, out_specs=P(None, "rhs", "leaf"), check_vma=False
    )
```

time: 32.6 us -> 26.3 us (0.81)
  blocking collectives: 16 us -> 0 us
  Pallas kernels: 13.6 us -> 24.3 us
  local copies, waits for them, and re-layouts: 2.77 us -> 1.87 us
    all_to_all x1 -> x0, blocking collectives: 16 us -> none  [per_device(): lax.all_to_all(state, 'leaf', split_axis=0, concat_axis=0, tiled=True)]
    pallas_call x2 -> x1, Pallas kernels: 13.6 us -> 24.3 us  [per_device(): pl.pallas_call(functools.partial(fused_kernel, count, chunks, near_levels...]
    reshape x1 -> x0, local copies, waits for them, and re-layouts: 2.75 us -> none  [per_device(): transfer = transfer.reshape(levels, 2, 2, rank, 2 * rank)]
    unnamed x10 -> x1, local copies, waits for them, and re-layouts: 0.02 us -> 1.87 us
where the time goes in v2:
time: 26.3 us; the launch traced here: 26.1 us
  Pallas kernels  24.3 us (92%)
  local copies, waits for them, and re-layouts  1.87 us (7%)
    pallas_call x1, Pallas kernels, per_device(): pl.pallas_call(functools.partial(fused_kernel, count, chunks, near_levels...  24.3 us
    unnamed x1, local copies, waits for them, and re-layouts  1.87 us

profile of v2, /device:TPU:0, one launch (start us, length us, event | category | flops | bytes accessed | tf_op | source)
XLA Modules:
  0.0 26.1 jit_solution(8475930344024305767)
XLA Ops:
  0.0 24.3 %fused.1 = f32[2,8,8192]{2,1,0:T(8,128)} custom-call(bf16[2,8,8192]{2,1,0:T(8,128)(2,1)} %exc_ref.1, f32[1,8192]{1,0:T(1,128)} %bitcast.4, s32[1,8192]{1,0:T(1,128)} %bitcast.5, bf16[2,64,64]{2,1,0:T(8,128)(2,1)} %leaf_ref.1, bf16[10,2,2,128,64]{4,3,2,1,0:T(8,128)(2,1)} %bitcast.3, bf16[2,64,64]{2,1,0:T(8,128)(2,1)} %eval_ref.1), custom_call_target="tpu_custom_call" | custom-call | tf_op jit(solution)/shard_map/fused/pallas_call | solution.py:285
  24.3 1.9 %copy.8 = f32[2,8,8192]{2,1,0:T(8,128)} copy(f32[2,8,8192]{2,1,0:T(8,128)} %fused.1) | data formatting | bytes 1048576

commit v3 on v2

--- a/solution.py
+++ b/solution.py
@@ -8,6 +8,9 @@
 
 LANES = 256
 CHUNKS = 2
+UNROLL = 8
+GROUP = 8
+SPLIT_BYTES = 32 * 1024 * 1024
 VMEM_BYTES = 56 * 1024 * 1024
 
 
@@ -146,9 +149,9 @@
             ]
 
 
-def fused_kernel(count, chunks, near_levels, exc_ref, weight_ref, order_ref, leaf_ref, transfer_ref,
-                 eval_ref, out_ref, weighted, pairs, hot, mats, halves, sent, held, values, total,
-                 send_sems, recv_sems):
+def send_kernel(count, chunks, near_levels, unroll, exc_ref, weight_ref, order_ref, leaf_ref,
+                transfer_ref, eval_ref, held, hot, far_mats, weighted, pairs, mats, halves, sent,
+                send_sems, recv_sems):
     vecs, points = exc_ref.shape[1:]
     levels = transfer_ref.shape[0]
     blocks = points // LANES
@@ -162,9 +165,10 @@
     weigh(exc_ref, weight_ref, weighted)
     for level in range(near_levels):
         mats[level] = level_matrix(transfer_ref, level, halves)
-    mats[levels] = leaf_matrix(leaf_ref)
+    mats[near_levels] = leaf_matrix(leaf_ref)
     steps = blocks // chunks
-    rows = sent.shape[2]
+    sources, rows, width = held.shape[1:]
+    sources //= chunks
     copies = []
     for chunk in range(chunks):
 
@@ -172,22 +176,24 @@
             gather_step(chunk * steps + step, vecs, blocks, order_ref, weighted, hot, pairs)
             return carry
 
-        lax.fori_loop(0, steps, gather, 0, unroll=2)
+        lax.fori_loop(0, steps, gather, 0, unroll=min(unroll, steps))
         start = chunk * steps * 2 * vecs
-        joined = dot_rows(pairs[start : start + steps * 2 * vecs, :], mats[levels]).astype(
+        joined = dot_rows(pairs[start : start + steps * 2 * vecs, :], mats[near_levels]).astype(
             jnp.bfloat16
         )
         for level in range(near_levels):
             state = children(dot_rows(joined, mats[level]), vecs)
             if level + 1 < near_levels:
                 joined = pair_up(state, 2 << level, vecs)
-        sent[chunk] = state.reshape(count, rows, state.shape[1])
+        state = state.reshape(sources, count, rows, width)
+        for peer in range(count):
+            sent[chunk, peer] = state[:, peer]
         if chunk == 0:
             pl.semaphore_wait(barrier, count - 1)
         for hop, peer in peers:
             copy = pltpu.make_async_remote_copy(
                 src_ref=sent.at[chunk, peer],
-                dst_ref=held.at[me * chunks + chunk],
+                dst_ref=held.at[me, pl.ds(chunk * sources, sources)],
                 send_sem=send_sems.at[chunk, hop],
                 recv_sem=recv_sems.at[chunk, hop],
                 device_id={"leaf": peer},
@@ -195,20 +201,25 @@
             )
             copy.start()
             copies.append(copy)
-        held[me * chunks + chunk] = sent[chunk, me]
+        held[me, chunk * sources : (chunk + 1) * sources] = sent[chunk, me]
     for level in range(near_levels, levels):
-        mats[level] = level_matrix(transfer_ref, level, halves)
-    mats[levels + 1] = eval_matrix(eval_ref)
-    total[...] = jnp.zeros_like(total)
+        far_mats[level - near_levels] = level_matrix(transfer_ref, level, halves)
+    far_mats[levels - near_levels] = eval_matrix(eval_ref)
     for copy in copies:
         copy.wait()
-    state = held[...].reshape(count * chunks * rows, held.shape[2])
+
+
+def merge_kernel(vecs, group, held, hot, far_mats, order_ref, out_ref, values, total):
+    blocks = order_ref.shape[1] // LANES
+    count, sources, rows, width = held.shape
     targets = rows // vecs
-    for level in range(near_levels, levels):
-        state = children(dot_rows(pair_up(state, targets, vecs), mats[level]), vecs)
+    far_levels = far_mats.shape[0] - 1
+    state = held[...].reshape(count * sources * rows, width)
+    for level in range(far_levels):
+        state = children(dot_rows(pair_up(state, targets, vecs), far_mats[level]), vecs)
         targets *= 2
-    values[...] = dot_rows(pair_up(state, 1, vecs), mats[levels + 1])
-    group = 2
+    values[...] = dot_rows(pair_up(state, 1, vecs), far_mats[far_levels])
+    total[...] = jnp.zeros_like(total)
 
     def scatter(step, carry):
         scatter_steps(step, vecs, blocks, group, order_ref, hot, values, total)
@@ -276,35 +287,47 @@
     total = pltpu.VMEM((blocks * 2 * vecs, LANES), jnp.float32)
     hot = pltpu.VMEM((blocks, LANES, LANES), jnp.bfloat16)
     halves = pltpu.VMEM((2, 2, 2 * rank, rank), jnp.float32)
+    near_levels = (16 * count // vecs).bit_length() - 1
     chunks = CHUNKS
-    while chunks > 1 and boxes // chunks // count * vecs < 16:
+    while chunks > 1 and boxes // chunks < 1 << near_levels:
         chunks //= 2
-    rows = boxes // chunks // count * vecs
-    if rows >= 16:
-        near_levels = box_levels - (chunks.bit_length() - 1)
-        return pl.pallas_call(
-            functools.partial(fused_kernel, count, chunks, near_levels),
-            out_shape=out_shape,
-            in_specs=[pl.BlockSpec(memory_space=pltpu.VMEM)] * 6,
-            out_specs=pl.BlockSpec(memory_space=pltpu.VMEM),
+    if near_levels < box_levels:
+        sources = boxes >> near_levels
+        rows = boxes * vecs // (count * sources)
+        far_count = levels - near_levels + 1
+        vmem = pl.BlockSpec(memory_space=pltpu.VMEM)
+        held, table, far_mats = pl.pallas_call(
+            functools.partial(send_kernel, count, chunks, near_levels, UNROLL),
+            out_shape=[
+                jax.ShapeDtypeStruct((count, sources, rows, 2 * rank), jnp.bfloat16),
+                jax.ShapeDtypeStruct((blocks, LANES, LANES), jnp.bfloat16),
+                jax.ShapeDtypeStruct((far_count, 4 * rank, 4 * rank), jnp.bfloat16),
+            ],
+            in_specs=[vmem] * 6,
+            out_specs=[vmem] * 3,
             scratch_shapes=[
                 weighted,
                 pairs,
-                hot,
-                pltpu.VMEM((levels + 2, 4 * rank, 4 * rank), jnp.bfloat16),
+                pltpu.VMEM((near_levels + 1, 4 * rank, 4 * rank), jnp.bfloat16),
                 halves,
-                pltpu.VMEM((chunks, count, rows, 2 * rank), jnp.bfloat16),
-                pltpu.VMEM((count * chunks, rows, 2 * rank), jnp.bfloat16),
-                values,
-                total,
+                pltpu.VMEM((chunks, count, sources // chunks, rows, 2 * rank), jnp.bfloat16),
                 pltpu.SemaphoreType.DMA((chunks, count)),
                 pltpu.SemaphoreType.DMA((chunks, count)),
             ],
             compiler_params=pltpu.CompilerParams(
-                vmem_limit_bytes=VMEM_BYTES, collective_id=0, has_side_effects=True
+                vmem_limit_bytes=SPLIT_BYTES, collective_id=0, has_side_effects=True
             ),
-            name="fused",
+            name="send",
         )(excitation, weight_row, order_row, leaf_basis, transfer, eval_basis)
+        return pl.pallas_call(
+            functools.partial(merge_kernel, vecs, min(GROUP, blocks)),
+            out_shape=out_shape,
+            in_specs=[vmem] * 4,
+            out_specs=vmem,
+            scratch_shapes=[values, total],
+            compiler_params=pltpu.CompilerParams(vmem_limit_bytes=SPLIT_BYTES),
+            name="merge",
+        )(held, table, far_mats, order_row)
     params = pltpu.CompilerParams(vmem_limit_bytes=VMEM_BYTES)
     state = pl.pallas_call(
         functools.partial(near_kernel, box_levels),

time: 26.3 us -> 23.6 us (0.90)
  Pallas kernels: 24.3 us -> 17.9 us
  local copies, waits for them, and re-layouts: 1.87 us -> 5.29 us
    pallas_call x1 -> x2, Pallas kernels: 24.3 us -> 17.9 us  [the longest x1 12.9 us: per_device(): pl.pallas_call(functools.partial(send_kernel, count, chunks, near_levels,...]
    unnamed x1 -> x12, local copies, waits for them, and re-layouts: 1.87 us -> 5.29 us
where the time goes in v3:
time: 23.6 us; the launch traced here: 23.2 us
  Pallas kernels  17.9 us (76%)
  local copies, waits for them, and re-layouts  5.29 us (22%)
    pallas_call x1, Pallas kernels, per_device(): pl.pallas_call(functools.partial(send_kernel, count, chunks, near_levels,...  12.9 us
    unnamed x12, local copies, waits for them, and re-layouts  5.29 us
    pallas_call x1, Pallas kernels, per_device(): pl.pallas_call(functools.partial(merge_kernel, vecs, min(GROUP, blocks)),...  4.94 us

profile of v3, /device:TPU:0, one launch (start us, length us, event | category | flops | bytes accessed | tf_op | source)
XLA Modules:
  0.0 23.2 jit_solution(9729914447882747523)
XLA Ops:
  0.0 0.0 copy-start
  0.0 1.3 %copy-done = bf16[10,2,2,64,2,64]{5,4,3,2,1,0:T(2,128)(2,1)S(1)} copy-done((bf16[10,2,2,64,2,64]{5,4,3,2,1,0:T(2,128)(2,1)S(1)}, bf16[10,2,2,64,2,64]{5,4,3,2,1,0:T(2,128)(2,1)}, u32[]{:S(2)}) %copy-start) | copy-done | bytes 655384
  1.3 0.0 copy-start.1
  1.3 0.9 %copy-done.1 = bf16[2,8,8192]{2,1,0:T(8,128)(2,1)S(1)} copy-done((bf16[2,8,8192]{2,1,0:T(8,128)(2,1)S(1)}, bf16[2,8,8192]{2,1,0:T(8,128)(2,1)}, u32[]{:S(2)}) %copy-start.1) | copy-done | bytes 262168
  2.3 0.0 copy-start.2
  2.3 0.8 %copy-done.2 = s32[8192]{0:T(1024)S(1)} copy-done((s32[8192]{0:T(1024)S(1)}, s32[8192]{0:T(1024)}, u32[]{:S(2)}) %copy-start.2) | copy-done | bytes 32792
  3.0 0.0 copy-start.3
  3.0 0.8 %copy-done.3 = f32[8192]{0:T(1024)S(1)} copy-done((f32[8192]{0:T(1024)S(1)}, f32[8192]{0:T(1024)}, u32[]{:S(2)}) %copy-start.3) | copy-done | bytes 32792
  3.8 0.0 copy-start.4
  3.8 0.8 %copy-done.4 = bf16[2,64,64]{2,1,0:T(8,128)(2,1)S(1)} copy-done((bf16[2,64,64]{2,1,0:T(8,128)(2,1)S(1)}, bf16[2,64,64]{2,1,0:T(8,128)(2,1)}, u32[]{:S(2)}) %copy-start.4) | copy-done | bytes 16408
  4.5 0.0 copy-start.5
  4.5 0.8 %copy-done.5 = bf16[2,64,64]{2,1,0:T(8,128)(2,1)S(1)} copy-done((bf16[2,64,64]{2,1,0:T(8,128)(2,1)S(1)}, bf16[2,64,64]{2,1,0:T(8,128)(2,1)}, u32[]{:S(2)}) %copy-start.5) | copy-done | bytes 16408
  5.3 12.9 %send.1 = (bf16[8,8,16,128]{3,2,1,0:T(8,128)(2,1)S(1)}, bf16[32,256,256]{2,1,0:T(8,128)(2,1)S(1)}, bf16[7,256,256]{2,1,0:T(8,128)(2,1)S(1)}) custom-call(bf16[2,8,8192]{2,1,0:T(8,128)(2,1)S(1)} %copy-done.1, f32[1,8192]{1,0:T(1,128)S(1)} %bitcast.6, s32[1,8192]{1,0:T(1,128)S(1)} %bitcast.4, bf16[2,64,64]{2,1,0:T(8,128)(2,1)S(1)} %copy-done.4, ...), custom_call_target="tpu_custom_call" | custom-call | tf_op jit(solution)/shard_map/send/pallas_call | solution.py:299
  18.3 4.9 %merge.1 = f32[2,8,8192]{2,1,0:T(8,128)} custom-call(bf16[8,8,16,128]{3,2,1,0:T(8,128)(2,1)S(1)} %get-tuple-element.8.held, bf16[32,256,256]{2,1,0:T(8,128)(2,1)S(1)} %get-tuple-element.9.hot, bf16[7,256,256]{2,1,0:T(8,128)(2,1)S(1)} %get-tuple-element.10.far_mats, s32[1,8192]{1,0:T(1,128)S(1)} %bitcast.5), custom_call_target="tpu_custom_call" | custom-call | tf_op jit(solution)/shard_map/merge/pallas_call | solution.py:322
Async XLA Ops:
  0.0 1.3 %copy-start = (bf16[10,2,2,64,2,64]{5,4,3,2,1,0:T(2,128)(2,1)S(1)}, bf16[10,2,2,64,2,64]{5,4,3,2,1,0:T(2,128)(2,1)}, u32[]{:S(2)}) copy-start(bf16[10,2,2,64,2,64]{5,4,3,2,1,0:T(2,128)(2,1)} %param.10) | copy-start | bytes 1966084
  1.3 0.9 %copy-start.1 = (bf16[2,8,8192]{2,1,0:T(8,128)(2,1)S(1)}, bf16[2,8,8192]{2,1,0:T(8,128)(2,1)}, u32[]{:S(2)}) copy-start(bf16[2,8,8192]{2,1,0:T(8,128)(2,1)} %exc_ref.1) | copy-start | bytes 786436
  2.3 0.8 %copy-start.2 = (s32[8192]{0:T(1024)S(1)}, s32[8192]{0:T(1024)}, u32[]{:S(2)}) copy-start(s32[8192]{0:T(1024)} %param.8) | copy-start | bytes 98308
  3.0 0.8 %copy-start.3 = (f32[8192]{0:T(1024)S(1)}, f32[8192]{0:T(1024)}, u32[]{:S(2)}) copy-start(f32[8192]{0:T(1024)} %param.7) | copy-start | bytes 98308
  3.8 0.8 %copy-start.4 = (bf16[2,64,64]{2,1,0:T(8,128)(2,1)S(1)}, bf16[2,64,64]{2,1,0:T(8,128)(2,1)}, u32[]{:S(2)}) copy-start(bf16[2,64,64]{2,1,0:T(8,128)(2,1)} %leaf_ref.1) | copy-start | bytes 49156
  4.5 0.8 %copy-start.5 = (bf16[2,64,64]{2,1,0:T(8,128)(2,1)S(1)}, bf16[2,64,64]{2,1,0:T(8,128)(2,1)}, u32[]{:S(2)}) copy-start(bf16[2,64,64]{2,1,0:T(8,128)(2,1)} %eval_ref.1) | copy-start | bytes 49156

commit v4 on v3

--- a/solution.py
+++ b/solution.py
@@ -10,7 +10,6 @@
 CHUNKS = 2
 UNROLL = 8
 GROUP = 8
-SPLIT_BYTES = 32 * 1024 * 1024
 VMEM_BYTES = 56 * 1024 * 1024
 
 
@@ -144,17 +143,51 @@
     for block in range(blocks):
         rows = block * 2 * vecs
         for part in range(2):
-            out_ref[part, :, pl.ds(block * LANES, LANES)] = total[
-                pl.ds(rows + part * vecs, vecs), :
-            ]
-
-
-def send_kernel(count, chunks, near_levels, unroll, exc_ref, weight_ref, order_ref, leaf_ref,
-                transfer_ref, eval_ref, held, hot, far_mats, weighted, pairs, mats, halves, sent,
-                send_sems, recv_sems):
+            held = total[pl.ds(rows + part * vecs, vecs), :]
+            out_ref[part, :, pl.ds(block * LANES, LANES)] = held.astype(out_ref.dtype)
+
+
+def merge(vecs, group, held, hot, far_mats, order_ref, out_ref, values, total):
+    blocks = order_ref.shape[1] // LANES
+    count, sources, rows, width = held.shape
+    targets = rows // vecs
+    far_levels = far_mats.shape[0] - 1
+    state = held[...].reshape(count * sources * rows, width)
+    for level in range(far_levels):
+        state = children(dot_rows(pair_up(state, targets, vecs), far_mats[level]), vecs)
+        targets *= 2
+    values[...] = dot_rows(pair_up(state, 1, vecs), far_mats[far_levels])
+
+    def scatter(step, carry):
+        scatter_steps(step, vecs, blocks, group, order_ref, hot, values, total)
+        return carry
+
+    lax.fori_loop(0, blocks // group, scatter, 0)
+    write_out(vecs, blocks, total, out_ref)
+
+
+def fused_kernel(count, chunks, near_levels, unroll, group, exc_hbm, weight_hbm, order_hbm, leaf_hbm,
+                transfer_hbm, eval_hbm, out_ref, held, hot, far_mats, exc_ref, weight_ref,
+                order_ref, leaf_ref, transfer_ref, eval_ref, weighted, pairs, mats, halves, sent, values,
+                total, load_sems, send_sems, recv_sems):
     vecs, points = exc_ref.shape[1:]
     levels = transfer_ref.shape[0]
     blocks = points // LANES
+    loads = [
+        pltpu.make_async_copy(source, target, load_sems.at[index])
+        for index, (source, target) in enumerate(
+            [
+                (exc_hbm, exc_ref),
+                (weight_hbm, weight_ref),
+                (order_hbm, order_ref),
+                (transfer_hbm, transfer_ref),
+                (leaf_hbm, leaf_ref),
+                (eval_hbm, eval_ref),
+            ]
+        )
+    ]
+    for load in loads:
+        load.start()
     me = lax.axis_index("leaf")
     peers = [(hop, lax.rem(me + hop, count)) for hop in range(1, count)]
     barrier = pltpu.get_barrier_semaphore()
@@ -162,21 +195,33 @@
         pl.semaphore_signal(
             barrier, inc=1, device_id={"leaf": peer}, device_id_type=pl.DeviceIdType.MESH
         )
+    steps = blocks // chunks
+    unroll = min(unroll, steps)
+    groups = steps // unroll
+    inside = near_levels // groups
+    loads[0].wait()
+    loads[1].wait()
     weigh(exc_ref, weight_ref, weighted)
-    for level in range(near_levels):
-        mats[level] = level_matrix(transfer_ref, level, halves)
+    for load in loads[2:]:
+        load.wait()
+    for level in range(inside * groups, near_levels):
+        mats[level] = level_matrix(transfer_ref, level, halves.at[0])
     mats[near_levels] = leaf_matrix(leaf_ref)
-    steps = blocks // chunks
     sources, rows, width = held.shape[1:]
     sources //= chunks
     copies = []
     for chunk in range(chunks):
 
-        def gather(step, carry):
-            gather_step(chunk * steps + step, vecs, blocks, order_ref, weighted, hot, pairs)
+        def gather(round, carry):
+            for inner in range(unroll):
+                step = chunk * steps + round * unroll + inner
+                gather_step(step, vecs, blocks, order_ref, weighted, hot, pairs)
+                if chunk == 0 and inner < inside:
+                    level = round * inside + inner
+                    mats[level] = level_matrix(transfer_ref, level, halves.at[inner % 2])
             return carry
 
-        lax.fori_loop(0, steps, gather, 0, unroll=min(unroll, steps))
+        lax.fori_loop(0, groups, gather, 0)
         start = chunk * steps * 2 * vecs
         joined = dot_rows(pairs[start : start + steps * 2 * vecs, :], mats[near_levels]).astype(
             jnp.bfloat16
@@ -203,30 +248,12 @@
             copies.append(copy)
         held[me, chunk * sources : (chunk + 1) * sources] = sent[chunk, me]
     for level in range(near_levels, levels):
-        far_mats[level - near_levels] = level_matrix(transfer_ref, level, halves)
+        far_mats[level - near_levels] = level_matrix(transfer_ref, level, halves.at[level % 2])
     far_mats[levels - near_levels] = eval_matrix(eval_ref)
+    total[...] = jnp.zeros_like(total)
     for copy in copies:
         copy.wait()
-
-
-def merge_kernel(vecs, group, held, hot, far_mats, order_ref, out_ref, values, total):
-    blocks = order_ref.shape[1] // LANES
-    count, sources, rows, width = held.shape
-    targets = rows // vecs
-    far_levels = far_mats.shape[0] - 1
-    state = held[...].reshape(count * sources * rows, width)
-    for level in range(far_levels):
-        state = children(dot_rows(pair_up(state, targets, vecs), far_mats[level]), vecs)
-        targets *= 2
-    values[...] = dot_rows(pair_up(state, 1, vecs), far_mats[far_levels])
-    total[...] = jnp.zeros_like(total)
-
-    def scatter(step, carry):
-        scatter_steps(step, vecs, blocks, group, order_ref, hot, values, total)
-        return carry
-
-    lax.fori_loop(0, blocks // group, scatter, 0)
-    write_out(vecs, blocks, total, out_ref)
+    merge(vecs, group, held, hot, far_mats, order_ref, out_ref, values, total)
 
 
 def near_kernel(near_levels, exc_ref, weight_ref, order_ref, leaf_ref, transfer_ref,
@@ -295,39 +322,37 @@
         sources = boxes >> near_levels
         rows = boxes * vecs // (count * sources)
         far_count = levels - near_levels + 1
-        vmem = pl.BlockSpec(memory_space=pltpu.VMEM)
-        held, table, far_mats = pl.pallas_call(
-            functools.partial(send_kernel, count, chunks, near_levels, UNROLL),
-            out_shape=[
-                jax.ShapeDtypeStruct((count, sources, rows, 2 * rank), jnp.bfloat16),
-                jax.ShapeDtypeStruct((blocks, LANES, LANES), jnp.bfloat16),
-                jax.ShapeDtypeStruct((far_count, 4 * rank, 4 * rank), jnp.bfloat16),
-            ],
-            in_specs=[vmem] * 6,
-            out_specs=[vmem] * 3,
+        return pl.pallas_call(
+            functools.partial(fused_kernel, count, chunks, near_levels, UNROLL, min(GROUP, blocks)),
+            out_shape=jax.ShapeDtypeStruct((2, vecs, points), jnp.bfloat16),
+            in_specs=[pl.BlockSpec(memory_space=pltpu.HBM)] * 6,
+            out_specs=pl.BlockSpec(memory_space=pltpu.VMEM),
             scratch_shapes=[
+                pltpu.VMEM((count, sources, rows, 2 * rank), jnp.bfloat16),
+                hot,
+                pltpu.VMEM((far_count, 4 * rank, 4 * rank), jnp.bfloat16),
+                pltpu.VMEM(excitation.shape, excitation.dtype),
+                pltpu.VMEM(weight_row.shape, weight_row.dtype),
+                pltpu.VMEM(order_row.shape, order_row.dtype),
+                pltpu.VMEM(leaf_basis.shape, leaf_basis.dtype),
+                pltpu.VMEM(transfer.shape, transfer.dtype),
+                pltpu.VMEM(eval_basis.shape, eval_basis.dtype),
                 weighted,
                 pairs,
                 pltpu.VMEM((near_levels + 1, 4 * rank, 4 * rank), jnp.bfloat16),
-                halves,
+                pltpu.VMEM((2, 2, 2, 2 * rank, rank), jnp.float32),
                 pltpu.VMEM((chunks, count, sources // chunks, rows, 2 * rank), jnp.bfloat16),
+                values,
+                total,
+                pltpu.SemaphoreType.DMA((6,)),
                 pltpu.SemaphoreType.DMA((chunks, count)),
                 pltpu.SemaphoreType.DMA((chunks, count)),
             ],
             compiler_params=pltpu.CompilerParams(
-                vmem_limit_bytes=SPLIT_BYTES, collective_id=0, has_side_effects=True
+                vmem_limit_bytes=VMEM_BYTES, collective_id=0, has_side_effects=True
             ),
-            name="send",
-        )(excitation, weight_row, order_row, leaf_basis, transfer, eval_basis)
-        return pl.pallas_call(
-            functools.partial(merge_kernel, vecs, min(GROUP, blocks)),
-            out_shape=out_shape,
-            in_specs=[vmem] * 4,
-            out_specs=vmem,
-            scratch_shapes=[values, total],
-            compiler_params=pltpu.CompilerParams(vmem_limit_bytes=SPLIT_BYTES),
-            name="merge",
-        )(held, table, far_mats, order_row)
+            name="fused",
+        )(excitation, weight_row, order_row, leaf_basis, transfer, eval_basis).astype(jnp.float32)
     params = pltpu.CompilerParams(vmem_limit_bytes=VMEM_BYTES)
     state = pl.pallas_call(
         functools.partial(near_kernel, box_levels),

time: 23.6 us -> 21.1 us (0.89)
  local copies, waits for them, and re-layouts: 5.29 us -> 0 us
  other arithmetic: 0 us -> 1.78 us
  Pallas kernels: 17.9 us -> 19.1 us
    unnamed x12 -> x0, local copies, waits for them, and re-layouts: 5.29 us -> none
    convert_element_type x0 -> x1, other arithmetic: none -> 1.78 us  [per_device(): return pl.pallas_call(functools.partial(fused_kernel, count, chunks, near...]
    pallas_call x2 -> x1, Pallas kernels: 17.9 us -> 19.1 us  [per_device(): pl.pallas_call(functools.partial(fused_kernel, count, chunks, near_levels...]
where the time goes in v4:
time: 21.1 us; the launch traced here: 20.9 us
  Pallas kernels  19.1 us (91%)
  other arithmetic  1.78 us (8%)
    pallas_call x1, Pallas kernels, per_device(): pl.pallas_call(functools.partial(fused_kernel, count, chunks, near_levels...  19.1 us
    convert_element_type x1, other arithmetic, per_device(): return pl.pallas_call(functools.partial(fused_kernel, count, chunks, near...  1.78 us

profile of v4, /device:TPU:0, one launch (start us, length us, event | category | flops | bytes accessed | tf_op | source)
XLA Modules:
  0.0 20.9 jit_solution(12267813837151636649)
XLA Ops:
  0.0 19.1 %fused.1 = bf16[2,8,8192]{2,1,0:T(8,128)(2,1)} custom-call(bf16[2,8,8192]{2,1,0:T(8,128)(2,1)} %exc_hbm.1, f32[1,8192]{1,0:T(1,128)} %bitcast.4, s32[1,8192]{1,0:T(1,128)} %bitcast.5, bf16[2,64,64]{2,1,0:T(8,128)(2,1)} %leaf_hbm.1, bf16[10,2,2,128,64]{4,3,2,1,0:T(8,128)(2,1)} %bitcast.3, bf16[2,64,64]{2,1,0:T(8,128)(2,1)} %eval_hbm.1), custom_call_target="tpu_custom_call" | custom-call | tf_op jit(solution)/shard_map/fused/pallas_call | solution.py:325
  19.1 1.8 %convert_element_type.3 = f32[2,8,8192]{2,1,0:T(8,128)} convert(bf16[2,8,8192]{2,1,0:T(8,128)(2,1)} %fused.1) | non-fusion elementwise | flops 131072 | bytes 786432 | tf_op jit(solution)/shard_map/convert_element_type | solution.py:355

commit v5 on v4

--- a/solution.py
+++ b/solution.py
@@ -9,7 +9,7 @@
 LANES = 256
 CHUNKS = 2
 UNROLL = 8
-GROUP = 8
+GROUP = 16
 VMEM_BYTES = 56 * 1024 * 1024
 
 
@@ -198,30 +198,37 @@
     steps = blocks // chunks
     unroll = min(unroll, steps)
     groups = steps // unroll
-    inside = near_levels // groups
+    inside = min(near_levels, unroll)
     loads[0].wait()
     loads[1].wait()
     weigh(exc_ref, weight_ref, weighted)
-    for load in loads[2:]:
-        load.wait()
-    for level in range(inside * groups, near_levels):
-        mats[level] = level_matrix(transfer_ref, level, halves.at[0])
-    mats[near_levels] = leaf_matrix(leaf_ref)
+    loads[2].wait()
     sources, rows, width = held.shape[1:]
     sources //= chunks
     copies = []
     for chunk in range(chunks):
 
-        def gather(round, carry):
+        def gather(round, build):
             for inner in range(unroll):
                 step = chunk * steps + round * unroll + inner
                 gather_step(step, vecs, blocks, order_ref, weighted, hot, pairs)
-                if chunk == 0 and inner < inside:
-                    level = round * inside + inner
-                    mats[level] = level_matrix(transfer_ref, level, halves.at[inner % 2])
+                if build and inner < inside:
+                    mats[inner] = level_matrix(transfer_ref, inner, halves.at[inner % 2])
+
+        def gather_round(round, carry):
+            gather(round, False)
             return carry
 
-        lax.fori_loop(0, groups, gather, 0)
+        if chunk == 0:
+            lax.fori_loop(0, groups - 1, gather_round, 0)
+            for load in loads[3:]:
+                load.wait()
+            mats[near_levels] = leaf_matrix(leaf_ref)
+            gather(groups - 1, True)
+            for level in range(inside, near_levels):
+                mats[level] = level_matrix(transfer_ref, level, halves.at[0])
+        else:
+            lax.fori_loop(0, groups, gather_round, 0)
         start = chunk * steps * 2 * vecs
         joined = dot_rows(pairs[start : start + steps * 2 * vecs, :], mats[near_levels]).astype(
             jnp.bfloat16

time: 21.1 us -> 20.1 us (0.953)
  Pallas kernels: 19.1 us -> 18.2 us
    pallas_call x1, Pallas kernels: 19.1 us -> 18.2 us  [per_device(): pl.pallas_call(functools.partial(fused_kernel, count, chunks, near_levels...]
where the time goes in v5:
time: 20.1 us; the launch traced here: 20 us
  Pallas kernels  18.2 us (91%)
  other arithmetic  1.78 us (9%)
    pallas_call x1, Pallas kernels, per_device(): pl.pallas_call(functools.partial(fused_kernel, count, chunks, near_levels...  18.2 us
    convert_element_type x1, other arithmetic, per_device(): return pl.pallas_call(functools.partial(fused_kernel, count, chunks, near...  1.78 us

profile of v5, /device:TPU:0, one launch (start us, length us, event | category | flops | bytes accessed | tf_op | source)
XLA Modules:
  0.0 20.0 jit_solution(15180722380349809192)
XLA Ops:
  0.0 18.2 %fused.1 = bf16[2,8,8192]{2,1,0:T(8,128)(2,1)} custom-call(bf16[2,8,8192]{2,1,0:T(8,128)(2,1)} %exc_hbm.1, f32[1,8192]{1,0:T(1,128)} %bitcast.4, s32[1,8192]{1,0:T(1,128)} %bitcast.5, bf16[2,64,64]{2,1,0:T(8,128)(2,1)} %leaf_hbm.1, bf16[10,2,2,128,64]{4,3,2,1,0:T(8,128)(2,1)} %bitcast.3, bf16[2,64,64]{2,1,0:T(8,128)(2,1)} %eval_hbm.1), custom_call_target="tpu_custom_call" | custom-call | tf_op jit(solution)/shard_map/fused/pallas_call | solution.py:332
  18.2 1.8 %convert_element_type.3 = f32[2,8,8192]{2,1,0:T(8,128)} convert(bf16[2,8,8192]{2,1,0:T(8,128)(2,1)} %fused.1) | non-fusion elementwise | flops 131072 | bytes 786432 | tf_op jit(solution)/shard_map/convert_element_type | solution.py:362
